TPU v7x, 256 devices: a whole 4x4x8 slice. The times are simulated.
256 devices in a mesh: row: 16 (over z_lo, y, core), col: 16 (over z_hi, x).
Axes of the slice: x: 4, y: 4, z: 8 (z_hi: 4, z_lo: 2; z = z_hi * 2 + z_lo), core: 2. Of those that a mesh axis runs over, the one named last changes fastest.
Arguments:
- states_now: float32 [40, 32768], P(None, ('col', 'row')), may hold values from -60 to 60
- states_next: float32 [40, 32768], P(None, ('row', 'col')), may hold values from -60 to 60
- states_last: float32 [40, 32768], P(None, ('col', 'row')), may hold values from -60 to 60
- payoff_now: bfloat16 [64, 32768], P(None, ('col', 'row')), may hold values from 0 to 2
- payoff_next: bfloat16 [64, 32768], P(None, ('row', 'col')), may hold values from 0 to 2
- payoff_last: bfloat16 [64, 32768], P(None, ('col', 'row')), may hold values from 0 to 2
Outputs:
- value_next: float32 [64, 32768], P(None, ('row', 'col'))
- value_now: float32 [64, 32768], P(None, ('col', 'row'))
All inputs are finite; a program needn't handle non-finite values.
Results may differ from a plain program's by a relative error of at most 0.0003.
Values sent between devices are 32-bit elements; how exact they have to be, the bound alone decides.
A program may use at most 128 MiB of HBM per device.

v0:
```python
import math
import jax
import jax.numpy as jnp
from jax import lax
from jax.sharding import PartitionSpec as P


def log_kernel(row_states, col_states, row_norms, col_norms):
    cross_term = lax.dot_general(
        row_states,
        col_states,
        (((0,), (0,)), ((), ())),
        precision=lax.Precision.HIGHEST,
        preferred_element_type=jnp.float32,
    )
    return cross_term - 0.5 * row_norms[:, None] - 0.5 * col_norms[None, :]


def log_blocks(row_states, col_states):
    factors, points = row_states.shape
    block_rows = math.gcd(points, 512)
    block_count = points // block_rows
    blocks = row_states.reshape(factors, block_count, block_rows).transpose(1, 0, 2)
    norms = jnp.sum(row_states * row_states, axis=0).reshape(block_count, block_rows)
    col_norms = jnp.sum(col_states * col_states, axis=0)

    def build(block_item):
        row_piece, piece_norms = block_item
        return log_kernel(row_piece, col_states, piece_norms, col_norms)

    return lax.map(build, (blocks, norms))


def local_stats(log_weight):
    col_peak = jnp.max(log_weight, axis=(0, 1))
    col_sum = jnp.sum(jnp.exp(log_weight - col_peak[None, None, :]), axis=(0, 1))
    return (col_peak, col_sum)


def stats_row(col_peak, col_sum):
    global_peak = lax.pmax(col_peak, "row")
    global_sum = lax.psum(col_sum * jnp.exp(col_peak - global_peak), "row")
    return (global_peak, global_sum)


def continuation(log_weight, later_value, col_peak, col_sum):
    scaled = (later_value / col_sum[None, :]).astype(jnp.bfloat16)

    def project(weight_block):
        kernel = jnp.exp(weight_block - col_peak[None, :]).astype(jnp.bfloat16)
        return lax.dot_general(
            scaled, kernel, (((1,), (1,)), ((), ())), preferred_element_type=jnp.float32
        )

    pieces = lax.map(project, log_weight)
    block_count, block_rows = (log_weight.shape[0], log_weight.shape[1])
    return pieces.transpose(1, 0, 2).reshape(scaled.shape[0], block_count * block_rows)


def per_device(states_now, states_next, states_last, payoff_now, payoff_next, payoff_last):
    later_states, later_values = (
        lax.all_gather(states_last, "row", axis=1, tiled=True),
        lax.all_gather(payoff_last.astype(jnp.float32), "row", axis=1, tiled=True),
    )
    next_rows = lax.all_gather(states_next, "col", axis=1, tiled=True)
    weights = log_blocks(next_rows, later_states)
    col_peak, col_sum = local_stats(weights)
    col_peak, col_sum = stats_row(col_peak, col_sum)
    partial_value = continuation(weights, later_values, col_peak, col_sum)
    own_next = lax.psum_scatter(partial_value, "col", scatter_dimension=1, tiled=True)
    value_next = jnp.maximum(payoff_next.astype(jnp.float32), own_next)
    now_rows = lax.all_gather(states_now, "col", axis=1, tiled=True)
    next_cols, value_cols = (
        lax.all_gather(states_next, "row", axis=1, tiled=True),
        lax.all_gather(value_next, "row", axis=1, tiled=True),
    )
    weights = log_blocks(now_rows, next_cols)
    col_peak, col_sum = local_stats(weights)
    col_peak, col_sum = stats_row(col_peak, col_sum)
    partial_value = continuation(weights, value_cols, col_peak, col_sum)
    own_block = lax.psum_scatter(partial_value, "col", scatter_dimension=1, tiled=True)
    value_now = jnp.maximum(payoff_now.astype(jnp.float32), own_block)
    return (value_next, value_now)


def solution(mesh):
    in_specs = (
        P(None, ("col", "row")),
        P(None, ("row", "col")),
        P(None, ("col", "row")),
        P(None, ("col", "row")),
        P(None, ("row", "col")),
        P(None, ("col", "row")),
    )
    out_specs = (P(None, ("row", "col")), P(None, ("col", "row")))
    return jax.shard_map(
        per_device, mesh=mesh, in_specs=in_specs, out_specs=out_specs, check_vma=False
    )
```

profile of v0, /device:TPU:8, one launch (start us, length us, event | category | flops | bytes accessed | tf_op | source)
XLA Modules:
  0.0 563.3 jit_solution(17174039601657234633)
XLA Ops:
  7.2 48.8 %all_gather.21 = f32[40,2048]{1,0:T(8,128)S(1)} all-gather(f32[40,128]{1,0:T(8,128)} %param.14), channel_id=1, replica_groups=mesh['row'=16,'col'=16] {'col'}, dimensions={1}, use_global_device_ids=true | all-gather | bytes 348160 | tf_op jit(solution)/shard_map/all_gather | solution.py:72
  56.2 17.5 %all_gather.22 = f32[40,2048]{1,0:T(8,128)S(1)} all-gather(f32[40,128]{1,0:T(8,128)} %param.15), channel_id=1, replica_groups=mesh['row'=16,'col'=16] {'row'}, dimensions={1}, use_global_device_ids=true | all-gather | bytes 348160 | tf_op jit(solution)/shard_map/all_gather | solution.py:74
  73.7 40.1 %all_gather.18 = f32[40,2048]{1,0:T(8,128)S(1)} all-gather(f32[40,128]{1,0:T(8,128)} %param.15), channel_id=1, replica_groups=mesh['row'=16,'col'=16] {'col'}, dimensions={1}, use_global_device_ids=true | all-gather | bytes 348160 | tf_op jit(solution)/shard_map/all_gather | solution.py:65
  114.1 7.8 %broadcast.49.clone.1 = f32[4,512,2048]{2,1,0:T(8,128)} broadcast(f32[]{:T(128)} %constant.47.clone.1), dimensions={} | broadcast | bytes 16777220 | tf_op jit(solution)/shard_map/broadcast.11
  122.0 21.0 %while.42 = (s32[]{:T(128)}, f32[4,512,2048]{2,1,0:T(8,128)}, f32[4,40,512]{2,0,1:T(4,128)S(1)}, f32[40,2048]{1,0:T(8,128)S(1)}, f32[4,512]{1,0:T(4,128)S(1)}, /*index=5*/f32[2048]{0:T(1024)S(1)}, s32[]{:T(128)}) while((s32[]{:T(128)}, f32[4,512,2048]{2,1,0:T(8,128)}, f32[4,40,512]{2,0,1:T(4,128)S(1)}, f32[40,2048]{1,0:T(8,128)S(1)}, ...), condition=%wide.region_14.15_spmd, body=%wide.region_13.14_spmd.sunk | while | flops 505416192 | bytes 4799061 | solution.py:31
  122.1 5.2 bitcast_dynamic-update-slice_fusion.5
  127.4 5.1 bitcast_dynamic-update-slice_fusion.5
  132.6 5.2 bitcast_dynamic-update-slice_fusion.5
  137.9 5.1 bitcast_dynamic-update-slice_fusion.5
  143.0 20.0 %all_gather.19 = f32[40,2048]{1,0:T(8,128)S(1)} all-gather(f32[40,128]{1,0:T(8,128)S(1)} %copy-done.1), channel_id=1, replica_groups=mesh['row'=16,'col'=16] {'row'}, dimensions={1}, use_global_device_ids=true | all-gather | bytes 348160 | tf_op jit(solution)/shard_map/all_gather | solution.py:62
  163.0 7.8 %broadcast.49.clone = f32[4,512,2048]{2,1,0:T(8,128)} broadcast(f32[]{:T(128)} %constant.47.clone.1), dimensions={} | broadcast | bytes 16777220 | tf_op jit(solution)/shard_map/broadcast.11
  170.9 21.0 %while.40 = (s32[]{:T(128)}, f32[4,512,2048]{2,1,0:T(8,128)}, f32[4,40,512]{2,0,1:T(4,128)S(1)}, f32[40,2048]{1,0:T(8,128)S(1)}, f32[4,512]{1,0:T(4,128)S(1)}, /*index=5*/f32[2048]{0:T(1024)S(1)}, s32[]{:T(128)}) while((s32[]{:T(128)}, f32[4,512,2048]{2,1,0:T(8,128)}, f32[4,40,512]{2,0,1:T(4,128)S(1)}, f32[40,2048]{1,0:T(8,128)S(1)}, ...), condition=%wide.region_3.4_spmd, body=%wide.region_2.3_spmd.sunk | while | flops 505416192 | bytes 4799061 | solution.py:31
  171.0 5.2 bitcast_dynamic-update-slice_fusion.4
  176.2 5.1 bitcast_dynamic-update-slice_fusion.4
  181.5 5.2 bitcast_dynamic-update-slice_fusion.4
  186.8 5.1 bitcast_dynamic-update-slice_fusion.4
  191.9 6.6 %reduce_max.19 = f32[2048]{0:T(1024)S(1)} reduce(f32[4,512,2048]{2,1,0:T(8,128)} %get-tuple-element.384, f32[]{:T(128)} %constant.48.clone.1), dimensions={0,1}, to_apply=%region_15.16 | reduce | flops 4192256 | bytes 16785412 | tf_op jit(solution)/shard_map/reduce_max | solution.py:35
  198.5 6.6 %reduce_max.18 = f32[2048]{0:T(1024)S(1)} reduce(f32[4,512,2048]{2,1,0:T(8,128)} %get-tuple-element.366, f32[]{:T(128)} %constant.48.clone.1), dimensions={0,1}, to_apply=%region_4.5 | reduce | flops 4192256 | bytes 16785412 | tf_op jit(solution)/shard_map/reduce_max | solution.py:35
  205.1 8.1 %exponential_reduce_fusion = f32[2048]{0:T(1024)S(1)} fusion(f32[4,512,2048]{2,1,0:T(8,128)} %get-tuple-element.384, f32[2048]{0:T(1024)S(1)} %reduce_max.19), kind=kLoop, calls=%fused_computation.24 | loop fusion | flops 8386560 | bytes 16793600 | tf_op jit(solution)/shard_map/reduce_sum | solution.py:36
  213.1 50.4 %all-reduce.1 = (f32[2048]{0:T(1024)S(1)}, f32[2048]{0:T(1024)S(1)}) all-reduce(f32[2048]{0:T(1024)S(1)} %reduce_max.18, f32[2048]{0:T(1024)S(1)} %reduce_max.19), channel_id=1, replica_groups=mesh['row'=16,'col'=16] {'row'}, use_global_device_ids=true, to_apply=%region_5.6 | all-reduce | flops 4096 | bytes 32768 | tf_op jit(solution)/shard_map/pmax | solution.py:41
  263.5 8.1 %exponential_reduce_fusion.1 = f32[2048]{0:T(1024)S(1)} fusion(f32[4,512,2048]{2,1,0:T(8,128)} %get-tuple-element.366, f32[2048]{0:T(1024)S(1)} %reduce_max.18), kind=kLoop, calls=%fused_computation.25 | loop fusion | flops 8386560 | bytes 16793600 | tf_op jit(solution)/shard_map/reduce_sum | solution.py:36
  271.6 21.7 %all_gather.20 = f32[64,2048]{1,0:T(8,128)S(1)} all-gather(f32[64,128]{1,0:T(8,128)S(1)} %convert_element_type.22), channel_id=1, replica_groups=mesh['row'=16,'col'=16] {'row'}, dimensions={1}, use_global_device_ids=true | all-gather | bytes 557056 | tf_op jit(solution)/shard_map/all_gather | solution.py:63
  293.3 50.4 %all-reduce = (f32[2048]{0:T(1024)S(1)}, f32[2048]{0:T(1024)S(1)}) all-reduce(f32[2048]{0:T(1024)S(1)} %get-tuple-element.185, f32[2048]{0:T(1024)S(1)} %get-tuple-element.184), channel_id=1, replica_groups=mesh['row'=16,'col'=16] {'row'}, use_global_device_ids=true, to_apply=%region_7.8 | all-reduce | flops 4096 | bytes 32768 | tf_op jit(solution)/shard_map/psum | solution.py:42
  343.8 11.9 %while.41 = (s32[]{:T(128)}, f32[4,64,512]{2,1,0:T(8,128)S(1)}, f32[4,512,2048]{2,1,0:T(8,128)}, f32[2048]{0:T(1024)S(1)}, bf16[64,2048]{1,0:T(8,128)(2,1)S(1)}, /*index=5*/s32[]{:T(128)}) while((s32[]{:T(128)}, f32[4,64,512]{2,1,0:T(8,128)S(1)}, f32[4,512,2048]{2,1,0:T(8,128)}, f32[2048]{0:T(1024)S(1)}, bf16[64,2048]{1,0:T(8,128)(2,1)S(1)}, ...), condition=%wide.region_9.10_spmd, body=%wide.region_8.9_spmd.sunk | while | flops 136314880 | bytes 4596805 | solution.py:55
  356.6 83.4 %reduce-scatter.3.cloned.1.call-done = f32[64,128]{1,0:T(8,128)} async-done(((f32[64,2048]{1,0:T(8,128)}), f32[64,128]{1,0:T(8,128)}) %reduce-scatter.3.cloned.1.call-update) | async-done | bytes 32784 | tf_op jit(solution)/shard_map/reduce_scatter | solution.py:70
  440.9 17.9 %all_gather.23 = f32[64,2048]{1,0:T(8,128)S(1)} all-gather(f32[64,128]{1,0:T(8,128)S(1)} %convert_maximum_fusion.1), channel_id=1, replica_groups=mesh['row'=16,'col'=16] {'row'}, dimensions={1}, use_global_device_ids=true | all-gather | bytes 557056 | tf_op jit(solution)/shard_map/all_gather | solution.py:75
  458.8 11.9 %while.43 = (s32[]{:T(128)}, f32[4,64,512]{2,1,0:T(8,128)S(1)}, f32[4,512,2048]{2,1,0:T(8,128)}, f32[2048]{0:T(1024)S(1)}, bf16[64,2048]{1,0:T(8,128)(2,1)S(1)}, /*index=5*/s32[]{:T(128)}) while((s32[]{:T(128)}, f32[4,64,512]{2,1,0:T(8,128)S(1)}, f32[4,512,2048]{2,1,0:T(8,128)}, f32[2048]{0:T(1024)S(1)}, bf16[64,2048]{1,0:T(8,128)(2,1)S(1)}, ...), condition=%wide.region_20.21_spmd, body=%wide.region_19.20_spmd.sunk | while | flops 136314880 | bytes 4596805 | solution.py:55
  458.8 3.0 fusion.41
  461.8 3.0 fusion.41
  464.8 3.0 fusion.41
  467.8 3.0 fusion.41
  471.6 83.5 %reduce-scatter.5.cloned.1.call-done = f32[64,128]{1,0:T(8,128)} async-done(((f32[64,2048]{1,0:T(8,128)}), f32[64,128]{1,0:T(8,128)}) %reduce-scatter.5.cloned.1.call-update) | async-done | bytes 32784 | tf_op jit(solution)/shard_map/reduce_scatter | solution.py:81
  (60 shorter events, 17.3 us)
Async XLA Ops:
  7.2 432.9 %reduce-scatter.3.cloned.1.call-start = ((), (), s32[]{:S(2)}) async-start(), calls=%async_computation.2 | async-start | bytes 557056 | tf_op jit(solution)/shard_map/reduce_scatter | solution.py:70
  114.1 28.9 %copy-start.1 = (f32[40,128]{1,0:T(8,128)S(1)}, f32[40,128]{1,0:T(8,128)}, u32[]{:S(2)}) copy-start(f32[40,128]{1,0:T(8,128)} %param.16) | copy-start | bytes 61444
  205.1 66.5 %copy-start.2 = (bf16[64,128]{1,0:T(8,128)(2,1)S(1)}, bf16[64,128]{1,0:T(8,128)(2,1)}, u32[]{:S(2)}) copy-start(bf16[64,128]{1,0:T(8,128)(2,1)} %param.19) | copy-start | bytes 49156
  271.6 168.5 %copy-start.3 = (bf16[64,128]{1,0:T(8,128)(2,1)S(1)}, bf16[64,128]{1,0:T(8,128)(2,1)}, u32[]{:S(2)}) copy-start(bf16[64,128]{1,0:T(8,128)(2,1)} %param.18) | copy-start | bytes 49156
  355.7 199.3 %copy-start.4 = (bf16[64,128]{1,0:T(8,128)(2,1)S(1)}, bf16[64,128]{1,0:T(8,128)(2,1)}, u32[]{:S(2)}) copy-start(bf16[64,128]{1,0:T(8,128)(2,1)} %param.17) | copy-start | bytes 49156
  356.6 198.5 %reduce-scatter.5.cloned.1.call-start = ((), (), s32[]{:S(2)}) async-start(), calls=%async_computation.3 | async-start | bytes 557056 | tf_op jit(solution)/shard_map/reduce_scatter | solution.py:81
  440.9 115.6 %copy-start = (f32[64,128]{1,0:T(8,128)}, f32[64,128]{1,0:T(8,128)S(1)}, u32[]{:S(2)}) copy-start(f32[64,128]{1,0:T(8,128)S(1)} %convert_maximum_fusion.1) | copy-start | bytes 98308
Sparse Core Ops, SparseCore 0:
  356.7 83.3 reduce-scatter.2
  471.7 83.3 reduce-scatter.4
where the time goes:
time: 564 us; the launch traced here: 563 us
  blocking collectives  267 us (47%)
  waiting for transfers between devices  167 us (30%)
  matrix products  64.8 us (11%)
  other arithmetic  31.9 us (6%)
  local copies, waits for them, and re-layouts  18.5 us (3%)
  between operations  14.2 us (3%)
    reduce_scatter x2, waiting for transfers between devices, per_device(): lax.psum_scatter(partial_value, 'col', scatter_dimension=1, tiled=True)  167 us
    psum x1, blocking collectives, stats_row(): global_sum = lax.psum(col_sum * jnp.exp(col_peak - global_peak), 'row')  50.4 us
    pmax x1, blocking collectives, stats_row(): global_peak = lax.pmax(col_peak, 'row')  50.4 us
    all_gather x1, blocking collectives, per_device(): now_rows = lax.all_gather(states_now, 'col', axis=1, tiled=True)  48.8 us
    dot_general x8, matrix products, log_kernel(): lax.dot_general(row_states, col_states, (((0,), (0,)), ((), ())), precisi...  41.2 us
    all_gather x1, blocking collectives, per_device(): next_rows = lax.all_gather(states_next, 'col', axis=1, tiled=True)  40.1 us
    dot_general x8, matrix products, project(): lax.dot_general(scaled, kernel, (((1,), (1,)), ((), ())), preferred_eleme...  23.7 us
    all_gather x1, blocking collectives, per_device(): lax.all_gather(payoff_last.astype(jnp.float32), 'row', axis=1, tiled=True)  21.7 us
  transfers between devices with their start and end apart: 2, of which 2 were waited for; matrix products, arithmetic and copies ran while one was open for 0% of the time, Pallas kernels for 0%

commit v1 on v0

--- a/solution.py
+++ b/solution.py
@@ -72,7 +72,9 @@
     now_rows = lax.all_gather(states_now, "col", axis=1, tiled=True)
     next_cols, value_cols = (
         lax.all_gather(states_next, "row", axis=1, tiled=True),
-        lax.all_gather(value_next, "row", axis=1, tiled=True),
+        jnp.concatenate(
+            lax.all_to_all(jnp.stack([value_next] * lax.axis_size("row")), "row", 0, 0), axis=1
+        ),
     )
     weights = log_blocks(now_rows, next_cols)
     col_peak, col_sum = local_stats(weights)

time: 564 us -> 559 us (level)
  blocking collectives: 267 us -> 261 us
    all_gather x1 -> x0, blocking collectives: 17.9 us -> none  [per_device(): lax.all_gather(value_next, 'row', axis=1, tiled=True)]
    all_to_all x0 -> x1, blocking collectives: none -> 12.2 us  [per_device(): lax.all_to_all(jnp.stack([value_next] * lax.axis_size('row')), 'row', 0, 0)]
    another operation x4 -> x5, local copies, waits for them, and re-layouts: 15.8 us -> 15.8 us
where the time goes in v1:
time: 559 us
  blocking collectives  261 us (47%)
  waiting for transfers between devices  168 us (30%)
  matrix products  64.8 us (12%)
  other arithmetic  31.9 us (6%)
  local copies, waits for them, and re-layouts  18.6 us (3%)
  between operations  14.2 us (3%)
    reduce_scatter x2, waiting for transfers between devices, per_device(): lax.psum_scatter(partial_value, 'col', scatter_dimension=1, tiled=True)  168 us
    psum x1, blocking collectives, stats_row(): global_sum = lax.psum(col_sum * jnp.exp(col_peak - global_peak), 'row')  50.4 us
    pmax x1, blocking collectives, stats_row(): global_peak = lax.pmax(col_peak, 'row')  50.4 us
    all_gather x1, blocking collectives, per_device(): now_rows = lax.all_gather(states_now, 'col', axis=1, tiled=True)  48.8 us
    dot_general x8, matrix products, log_kernel(): lax.dot_general(row_states, col_states, (((0,), (0,)), ((), ())), precisi...  41.2 us
    all_gather x1, blocking collectives, per_device(): next_rows = lax.all_gather(states_next, 'col', axis=1, tiled=True)  40.1 us
    dot_general x8, matrix products, project(): lax.dot_general(scaled, kernel, (((1,), (1,)), ((), ())), preferred_eleme...  23.7 us
    all_gather x1, blocking collectives, per_device(): lax.all_gather(payoff_last.astype(jnp.float32), 'row', axis=1, tiled=True)  21.7 us
  transfers between devices with their start and end apart: 2, of which 2 were waited for; matrix products, arithmetic and copies ran while one was open for 0% of the time, Pallas kernels for 0%

profile of v1, /device:TPU:8, one launch (start us, length us, event | category | flops | bytes accessed | tf_op | source)
XLA Modules:
  0.0 558.7 jit_solution(7923526798970736386)
XLA Ops:
  7.2 48.8 %all_gather.18 = f32[40,2048]{1,0:T(8,128)S(1)} all-gather(f32[40,128]{1,0:T(8,128)} %param.14), channel_id=1, replica_groups=mesh['row'=16,'col'=16] {'col'}, dimensions={1}, use_global_device_ids=true | all-gather | bytes 348160 | tf_op jit(solution)/shard_map/all_gather | solution.py:72
  56.2 17.5 %all_gather.19 = f32[40,2048]{1,0:T(8,128)S(1)} all-gather(f32[40,128]{1,0:T(8,128)} %param.15), channel_id=1, replica_groups=mesh['row'=16,'col'=16] {'row'}, dimensions={1}, use_global_device_ids=true | all-gather | bytes 348160 | tf_op jit(solution)/shard_map/all_gather | solution.py:74
  73.7 40.1 %all_gather.15 = f32[40,2048]{1,0:T(8,128)S(1)} all-gather(f32[40,128]{1,0:T(8,128)} %param.15), channel_id=1, replica_groups=mesh['row'=16,'col'=16] {'col'}, dimensions={1}, use_global_device_ids=true | all-gather | bytes 348160 | tf_op jit(solution)/shard_map/all_gather | solution.py:65
  114.1 7.8 %broadcast.51.clone.1 = f32[4,512,2048]{2,1,0:T(8,128)} broadcast(f32[]{:T(128)} %constant.47.clone.1), dimensions={} | broadcast | bytes 16777220 | tf_op jit(solution)/shard_map/broadcast.11
  122.0 21.0 %while.42 = (s32[]{:T(128)}, f32[4,512,2048]{2,1,0:T(8,128)}, f32[4,40,512]{2,0,1:T(4,128)S(1)}, f32[40,2048]{1,0:T(8,128)S(1)}, f32[4,512]{1,0:T(4,128)S(1)}, /*index=5*/f32[2048]{0:T(1024)S(1)}, s32[]{:T(128)}) while((s32[]{:T(128)}, f32[4,512,2048]{2,1,0:T(8,128)}, f32[4,40,512]{2,0,1:T(4,128)S(1)}, f32[40,2048]{1,0:T(8,128)S(1)}, ...), condition=%wide.region_14.15_spmd, body=%wide.region_13.14_spmd.sunk | while | flops 505416192 | bytes 4799061 | solution.py:31
  122.1 5.2 bitcast_dynamic-update-slice_fusion.5
  127.4 5.1 bitcast_dynamic-update-slice_fusion.5
  132.6 5.2 bitcast_dynamic-update-slice_fusion.5
  137.9 5.1 bitcast_dynamic-update-slice_fusion.5
  143.0 20.0 %all_gather.16 = f32[40,2048]{1,0:T(8,128)S(1)} all-gather(f32[40,128]{1,0:T(8,128)S(1)} %copy-done.1), channel_id=1, replica_groups=mesh['row'=16,'col'=16] {'row'}, dimensions={1}, use_global_device_ids=true | all-gather | bytes 348160 | tf_op jit(solution)/shard_map/all_gather | solution.py:62
  163.0 7.8 %broadcast.51.clone = f32[4,512,2048]{2,1,0:T(8,128)} broadcast(f32[]{:T(128)} %constant.47.clone.1), dimensions={} | broadcast | bytes 16777220 | tf_op jit(solution)/shard_map/broadcast.11
  170.9 21.0 %while.40 = (s32[]{:T(128)}, f32[4,512,2048]{2,1,0:T(8,128)}, f32[4,40,512]{2,0,1:T(4,128)S(1)}, f32[40,2048]{1,0:T(8,128)S(1)}, f32[4,512]{1,0:T(4,128)S(1)}, /*index=5*/f32[2048]{0:T(1024)S(1)}, s32[]{:T(128)}) while((s32[]{:T(128)}, f32[4,512,2048]{2,1,0:T(8,128)}, f32[4,40,512]{2,0,1:T(4,128)S(1)}, f32[40,2048]{1,0:T(8,128)S(1)}, ...), condition=%wide.region_3.4_spmd, body=%wide.region_2.3_spmd.sunk | while | flops 505416192 | bytes 4799061 | solution.py:31
  171.0 5.2 bitcast_dynamic-update-slice_fusion.4
  176.2 5.1 bitcast_dynamic-update-slice_fusion.4
  181.5 5.2 bitcast_dynamic-update-slice_fusion.4
  186.8 5.1 bitcast_dynamic-update-slice_fusion.4
  191.9 6.6 %reduce_max.19 = f32[2048]{0:T(1024)S(1)} reduce(f32[4,512,2048]{2,1,0:T(8,128)} %get-tuple-element.408, f32[]{:T(128)} %constant.48.clone.1), dimensions={0,1}, to_apply=%region_15.16 | reduce | flops 4192256 | bytes 16785412 | tf_op jit(solution)/shard_map/reduce_max | solution.py:35
  198.5 6.6 %reduce_max.18 = f32[2048]{0:T(1024)S(1)} reduce(f32[4,512,2048]{2,1,0:T(8,128)} %get-tuple-element.390, f32[]{:T(128)} %constant.48.clone.1), dimensions={0,1}, to_apply=%region_4.5 | reduce | flops 4192256 | bytes 16785412 | tf_op jit(solution)/shard_map/reduce_max | solution.py:35
  205.1 8.1 %exponential_reduce_fusion = f32[2048]{0:T(1024)S(1)} fusion(f32[4,512,2048]{2,1,0:T(8,128)} %get-tuple-element.408, f32[2048]{0:T(1024)S(1)} %reduce_max.19), kind=kLoop, calls=%fused_computation.24 | loop fusion | flops 8386560 | bytes 16793600 | tf_op jit(solution)/shard_map/reduce_sum | solution.py:36
  213.1 50.4 %all-reduce.1 = (f32[2048]{0:T(1024)S(1)}, f32[2048]{0:T(1024)S(1)}) all-reduce(f32[2048]{0:T(1024)S(1)} %reduce_max.18, f32[2048]{0:T(1024)S(1)} %reduce_max.19), channel_id=1, replica_groups=mesh['row'=16,'col'=16] {'row'}, use_global_device_ids=true, to_apply=%region_5.6 | all-reduce | flops 4096 | bytes 32768 | tf_op jit(solution)/shard_map/pmax | solution.py:41
  263.5 8.1 %exponential_reduce_fusion.1 = f32[2048]{0:T(1024)S(1)} fusion(f32[4,512,2048]{2,1,0:T(8,128)} %get-tuple-element.390, f32[2048]{0:T(1024)S(1)} %reduce_max.18), kind=kLoop, calls=%fused_computation.25 | loop fusion | flops 8386560 | bytes 16793600 | tf_op jit(solution)/shard_map/reduce_sum | solution.py:36
  271.6 21.7 %all_gather.17 = f32[64,2048]{1,0:T(8,128)S(1)} all-gather(f32[64,128]{1,0:T(8,128)S(1)} %convert_element_type.22), channel_id=1, replica_groups=mesh['row'=16,'col'=16] {'row'}, dimensions={1}, use_global_device_ids=true | all-gather | bytes 557056 | tf_op jit(solution)/shard_map/all_gather | solution.py:63
  293.3 50.4 %all-reduce = (f32[2048]{0:T(1024)S(1)}, f32[2048]{0:T(1024)S(1)}) all-reduce(f32[2048]{0:T(1024)S(1)} %get-tuple-element.209, f32[2048]{0:T(1024)S(1)} %get-tuple-element.208), channel_id=1, replica_groups=mesh['row'=16,'col'=16] {'row'}, use_global_device_ids=true, to_apply=%region_7.8 | all-reduce | flops 4096 | bytes 32768 | tf_op jit(solution)/shard_map/psum | solution.py:42
  343.8 11.9 %while.41 = (s32[]{:T(128)}, f32[4,64,512]{2,1,0:T(8,128)S(1)}, f32[4,512,2048]{2,1,0:T(8,128)}, f32[2048]{0:T(1024)S(1)}, bf16[64,2048]{1,0:T(8,128)(2,1)S(1)}, /*index=5*/s32[]{:T(128)}) while((s32[]{:T(128)}, f32[4,64,512]{2,1,0:T(8,128)S(1)}, f32[4,512,2048]{2,1,0:T(8,128)}, f32[2048]{0:T(1024)S(1)}, bf16[64,2048]{1,0:T(8,128)(2,1)S(1)}, ...), condition=%wide.region_9.10_spmd, body=%wide.region_8.9_spmd.sunk | while | flops 136314880 | bytes 4596805 | solution.py:55
  356.6 83.4 %reduce-scatter.3.cloned.1.call-done = f32[64,128]{1,0:T(8,128)} async-done(((f32[64,2048]{1,0:T(8,128)}), f32[64,128]{1,0:T(8,128)}) %reduce-scatter.3.cloned.1.call-update) | async-done | bytes 32784 | tf_op jit(solution)/shard_map/reduce_scatter | solution.py:70
  440.9 12.2 %all_to_all.5 = f32[16,64,128]{2,1,0:T(8,128)S(1)} all-to-all(f32[16,64,128]{2,1,0:T(8,128)S(1)} %stack.2), channel_id=1, replica_groups=mesh['row'=16,'col'=16] {'row'}, dimensions={0} | all-to-all | bytes 1048576 | tf_op jit(solution)/shard_map/all_to_all | solution.py:76
  453.2 11.9 %while.43 = (s32[]{:T(128)}, f32[4,64,512]{2,1,0:T(8,128)S(1)}, f32[4,512,2048]{2,1,0:T(8,128)}, f32[2048]{0:T(1024)S(1)}, bf16[64,2048]{1,0:T(8,128)(2,1)S(1)}, /*index=5*/s32[]{:T(128)}) while((s32[]{:T(128)}, f32[4,64,512]{2,1,0:T(8,128)S(1)}, f32[4,512,2048]{2,1,0:T(8,128)}, f32[2048]{0:T(1024)S(1)}, bf16[64,2048]{1,0:T(8,128)(2,1)S(1)}, ...), condition=%wide.region_20.21_spmd, body=%wide.region_19.20_spmd.sunk | while | flops 136314880 | bytes 4596805 | solution.py:55
  453.2 3.0 fusion.43
  456.1 3.0 fusion.43
  459.1 3.0 fusion.43
  462.1 3.0 fusion.43
  465.9 84.5 %reduce-scatter.5.cloned.1.call-done = f32[64,128]{1,0:T(8,128)} async-done(((f32[64,2048]{1,0:T(8,128)}), f32[64,128]{1,0:T(8,128)}) %reduce-scatter.5.cloned.1.call-update) | async-done | bytes 32784 | tf_op jit(solution)/shard_map/reduce_scatter | solution.py:83
  (61 shorter events, 17.3 us)
Async XLA Ops:
  7.2 432.9 %reduce-scatter.3.cloned.1.call-start = ((), (), s32[]{:S(2)}) async-start(), calls=%async_computation.3 | async-start | bytes 557056 | tf_op jit(solution)/shard_map/reduce_scatter | solution.py:70
  114.1 28.9 %copy-start.1 = (f32[40,128]{1,0:T(8,128)S(1)}, f32[40,128]{1,0:T(8,128)}, u32[]{:S(2)}) copy-start(f32[40,128]{1,0:T(8,128)} %param.16) | copy-start | bytes 61444
  205.1 66.5 %copy-start.2 = (bf16[64,128]{1,0:T(8,128)(2,1)S(1)}, bf16[64,128]{1,0:T(8,128)(2,1)}, u32[]{:S(2)}) copy-start(bf16[64,128]{1,0:T(8,128)(2,1)} %param.19) | copy-start | bytes 49156
  271.6 168.5 %copy-start.3 = (bf16[64,128]{1,0:T(8,128)(2,1)S(1)}, bf16[64,128]{1,0:T(8,128)(2,1)}, u32[]{:S(2)}) copy-start(bf16[64,128]{1,0:T(8,128)(2,1)} %param.18) | copy-start | bytes 49156
  355.7 194.7 %copy-start.4 = (bf16[64,128]{1,0:T(8,128)(2,1)S(1)}, bf16[64,128]{1,0:T(8,128)(2,1)}, u32[]{:S(2)}) copy-start(bf16[64,128]{1,0:T(8,128)(2,1)} %param.17) | copy-start | bytes 49156
  356.6 193.9 %reduce-scatter.5.cloned.1.call-start = ((), (), s32[]{:S(2)}) async-start(), calls=%async_computation.4 | async-start | bytes 557056 | tf_op jit(solution)/shard_map/reduce_scatter | solution.py:83
  440.9 111.0 %copy-start = (f32[64,128]{1,0:T(8,128)}, f32[64,128]{1,0:T(8,128)S(1)}, u32[]{:S(2)}) copy-start(f32[64,128]{1,0:T(8,128)S(1)} %convert_maximum_fusion.1) | copy-start | bytes 98308
Sparse Core Ops, SparseCore 0:
  356.7 83.3 reduce-scatter.2
  466.0 84.3 reduce-scatter.4
